TPU v7x, 32 devices: a whole 2x2x4 slice. The times are simulated.
32 devices in a mesh: groups: 2 (over x), shard: 16 (over z, y, core).
Axes of the slice: x: 2, y: 2, z: 4, core: 2. Of those that a mesh axis runs over, the one named last changes fastest.
Arguments:
- hidden: bfloat16 [8192, 8192], P(('groups', 'shard')), parts along dimension 0, may hold values from -6 to 6
- queries: bfloat16 [8192, 4096], P(('groups', 'shard')), parts along dimension 0, may hold values from -48 to 48
- segment: int32 [8192], P('groups'), parts along dimension 0, may hold values from 0 to 4095, as said below
- target_device: int32 [32], P('groups'), parts along dimension 0, may hold values from 0 to 15, as said below
- target_slot: int32 [32], P('groups'), parts along dimension 0, may hold values from 0 to 1, as said below
- key_codes: bfloat16 [8192, 512], P('shard'), may hold values from -0.0625 to 0.0625
- key_scales: float32 [64, 4], P('shard'), may hold values from 0.5 to 2
- value_codes: bfloat16 [8192, 512], P('shard'), may hold values from -0.0625 to 0.0625
- value_scales: float32 [64, 4], P('shard'), may hold values from 0.5 to 2
Outputs:
- attended: bfloat16 [16384, 4096], P(('groups', 'shard')), parts along dimension 0
There are 2 independent parts, one for each index of `groups`. A program takes and returns all parts, laid end to end along the dimension named above; an argument that names none is the same for every part. Nothing has to cross between parts.
Inputs may be any that keep to these rules, and one draw needn't show every extreme that they name: Block b, the 256 rows that shard index b holds, goes to shard index target_device[b], at most 1 places away counting cyclically. The blocks of one rollout all go to one device, in their cyclic order, to slots 0, 1, and so on; a device receives at most 2 blocks and at most one from each device. In every draw some device receives 2 blocks, and every displacement from -1 to 1 occurs. `target_slot`: blocks with one destination have distinct slots. `segment`: ids are distinct between rollouts, and both ends of the range occur in every draw. A rollout's rows lie in blocks that go to one device, in slot order then row order; a rollout has at most 512 rows, and one has that many in every draw.
All inputs are finite; a program needn't handle non-finite values.
Results may differ from a plain program's by a relative error of at most 0.012.
The roundings to bfloat16 on the way count: a program that leaves them out, or rounds other values in their place, can miss the bound.
Values may be sent and summed in bfloat16 or wider, within the bound.
A program may use at most 192 MiB of HBM per device.

v0:
```python
import jax
import jax.numpy as jnp
from jax import lax
from jax.sharding import PartitionSpec as P

KVH = 4
HD = 128
QPK = 8
QB = 128
CAP = 2
HOP = 1


def passed_along(block, axis, distance):
    devices = range(lax.axis_size(axis))
    route = [((i - distance) % len(devices), i) for i in devices]
    return lax.ppermute(block, axis, route)


def dequantize(codes, scales):
    row_count, col_count = codes.shape
    blocks = codes.astype(jnp.float32).reshape(row_count // QB, QB, col_count // QB, QB)
    scaled = blocks * scales[:, None, :, None]
    return scaled.reshape(row_count, col_count).astype(jnp.bfloat16)


def regroup(payload, target_device, target_slot):
    cycle_size = lax.axis_size("shard")
    own_index = lax.axis_index("shard")
    slot_ids = jnp.arange(CAP, dtype=jnp.int32)
    result = jnp.zeros((CAP,) + payload.shape, payload.dtype)
    for offset in range(-HOP, HOP + 1):
        if offset == 0:
            arrived = payload
        else:
            arrived = passed_along(payload, "shard", offset)
        source = (own_index - offset) % cycle_size
        landing = lax.dynamic_index_in_dim(target_device, source, keepdims=False) == own_index
        wanted = lax.dynamic_index_in_dim(target_slot, source, keepdims=False)
        chosen = jnp.logical_and(slot_ids == wanted, landing)
        result = jnp.where(chosen[:, None, None], arrived[None], result)
    return result.reshape(CAP * payload.shape[0], payload.shape[1])


def slot_segments(segment, target_device, target_slot):
    own_index = lax.axis_index("shard")
    block_count = target_device.shape[0]
    segment_rows = segment.reshape(block_count, -1)
    matches = jnp.logical_and(
        target_device[:, None] == own_index,
        target_slot[:, None] == jnp.arange(CAP, dtype=jnp.int32)[None, :],
    )
    summed = jnp.sum(jnp.where(matches[:, :, None], segment_rows[:, None, :], 0), axis=0)
    present = jnp.any(matches, axis=0)
    return jnp.where(present[:, None], summed, -1).reshape(-1)


def projector(hidden_rows, portion):
    return jnp.dot(hidden_rows, portion, preferred_element_type=jnp.float32)


def attend(query_rows, key_rows, value_rows, allowed):
    query_count = query_rows.shape[0]
    key_count = key_rows.shape[0]
    head_width = QPK * HD
    query_groups = query_rows.reshape(query_count, KVH, head_width).transpose(1, 0, 2)
    key_groups = key_rows.reshape(key_count, KVH, HD).transpose(1, 0, 2)
    value_groups = value_rows.reshape(key_count, KVH, HD).transpose(1, 0, 2)

    def one_group(operands):
        query_group, key_group, value_group = operands
        scores = jnp.einsum(
            "rqd,sd->qrs",
            query_group.reshape(query_count, QPK, HD),
            key_group,
            preferred_element_type=jnp.float32,
        ) * HD ** (-0.5)
        masked = jnp.where(allowed[None], scores, -1e30)
        row_max = jnp.max(masked, axis=-1, keepdims=True)
        raised = jnp.where(allowed[None], jnp.exp(masked - row_max), 0.0)
        weights = (raised / jnp.sum(raised, axis=-1, keepdims=True)).astype(jnp.bfloat16)
        mixed_rows = jnp.einsum(
            "qrs,sd->rqd", weights, value_group, preferred_element_type=jnp.float32
        )
        return mixed_rows.astype(jnp.bfloat16).reshape(query_count, head_width)

    outputs = lax.map(one_group, (query_groups, key_groups, value_groups))
    return outputs.transpose(1, 0, 2).reshape(query_count, KVH * head_width)


def per_device(
    hidden,
    queries,
    segment,
    target_device,
    target_slot,
    key_codes,
    key_scales,
    value_codes,
    value_scales,
):
    local_weights = jnp.concatenate(
        (dequantize(key_codes, key_scales), dequantize(value_codes, value_scales)), axis=1
    )
    pair_width = local_weights.shape[1]
    key_width = pair_width // 2
    block_rows = hidden.shape[0]
    slot_segment = slot_segments(segment, target_device, target_slot)
    projected = projector(hidden, lax.all_gather(local_weights, "shard", axis=0, tiled=True))
    key_value = projected.astype(jnp.bfloat16)
    cycle_size = lax.axis_size("shard")
    own_index = lax.axis_index("shard")
    segment_blocks = segment.reshape(cycle_size, block_rows)
    own_segment = lax.dynamic_index_in_dim(segment_blocks, own_index, keepdims=False)
    key_parts = [key_value]
    segment_parts = [own_segment]
    key_parts.append(passed_along(key_value, "shard", 1))
    segment_parts.append(
        lax.dynamic_index_in_dim(segment_blocks, (own_index - 1) % cycle_size, keepdims=False)
    )
    all_keys = jnp.concatenate(key_parts, axis=0)
    all_segments = jnp.concatenate(segment_parts, axis=0)
    row_index = jnp.arange(block_rows, dtype=jnp.int32)
    key_index = jnp.arange(all_keys.shape[0], dtype=jnp.int32)
    earlier = jnp.logical_or(
        key_index[None, :] >= block_rows, key_index[None, :] <= row_index[:, None]
    )
    allowed = jnp.logical_and(own_segment[:, None] == all_segments[None, :], earlier)
    own_result = attend(queries, all_keys[:, :key_width], all_keys[:, key_width:], allowed)
    attended = regroup(own_result, target_device, target_slot)
    return jnp.where(slot_segment[:, None] >= 0, attended, jnp.zeros_like(attended))


def solution(mesh):
    return jax.shard_map(
        per_device,
        mesh=mesh,
        in_specs=(
            P(("groups", "shard"), None),
            P(("groups", "shard"), None),
            P("groups"),
            P("groups"),
            P("groups"),
            P("shard", None),
            P("shard", None),
            P("shard", None),
            P("shard", None),
        ),
        out_specs=P(("groups", "shard"), None),
        check_vma=False,
    )
```

profile of v0, /device:TPU:1, one launch (start us, length us, event | category | flops | bytes accessed | tf_op | source)
XLA Modules:
  0.0 261.0 jit_solution(8931315545808995157)
XLA Ops:
  6.5 0.9 mul.28
  7.4 0.9 mul.31
  8.3 1.6 fusion.37
  9.9 1.1 pad_maximum_fusion
  11.0 0.0 all-gather.2.cloned.1.call-update
  11.1 0.0 copy-start
  11.1 129.5 %all-gather.2.cloned.1.call-done = bf16[8192,1024]{1,0:T(8,128)(2,1)} async-done(((bf16[512,1024]{1,0:T(8,128)(2,1)}), bf16[8192,1024]{1,0:T(8,128)(2,1)}) %all-gather.2.cloned.1.call-update) | async-done | bytes 16777232 | tf_op jit(solution)/shard_map/all_gather | solution.py:109
  140.6 11.5 %fusion.36 = bf16[256,1024]{1,0:T(8,128)(2,1)S(1)} fusion(bf16[256,8192]{1,0:T(8,128)(2,1)} %param.11, bf16[8192,1024]{1,0:T(8,128)(2,1)} %all-gather.2.cloned.1.call-done), kind=kOutput, calls=%fused_computation.34 | convolution fusion | flops 4295229440 | bytes 21495808 | tf_op jit(solution)/shard_map/dot_general | solution.py:59
  152.1 0.5 collective-permute-start
  152.6 3.3 %copy.28 = bf16[256,4096]{0,1:T(8,128)(2,1)S(1)} copy(bf16[256,4096]{1,0:T(8,128)(2,1)} %param.12) | data formatting | bytes 4194304 | tf_op args[1]
  156.0 2.8 %collective-permute-done = bf16[256,1024]{1,0:T(8,128)(2,1)} collective-permute-done((bf16[256,1024]{1,0:T(8,128)(2,1)S(1)}, bf16[256,1024]{1,0:T(8,128)(2,1)}, u32[]{:S(2)}, u32[]{:S(2)}) %collective-permute-start) | collective-permute-done | bytes 524320 | tf_op jit(solution)/shard_map/ppermute | solution.py:17
  158.7 1.1 fusion.40
  159.9 0.1 copy.41
  160.0 1.0 copy.34
  161.0 30.5 %while.11 = (s32[]{:T(128)}, bf16[4,256,1024]{1,2,0:T(8,128)(2,1)}, bf16[4,512,128]{1,2,0:T(8,128)(2,1)}, bf16[4,512,128]{2,1,0:T(8,128)(2,1)S(1)}, bf16[4,256,1...) while((s32[]{:T(128)}, bf16[4,256,1024]{1,2,0:T(8,128)(2,1)}, ...), condition=%wide.region_5.6_spmd.clone, body=%wide.region_2.5_spmd.clone.sunk | while | flops 544997888 | bytes 12209781 | solution.py:87
  161.0 0.2 fusion.62
  161.2 3.8 %fusion.63 = (f32[8,256]{1,0:T(8,128)S(1)}, f32[8,256,512]{1,2,0:T(8,128)}) fusion(pred[256,512]{0,1:T(8,128)(4,1)S(1)} %fusion.62, bf16[256,8,128]{0,2,1:T(8,128)(2,1)S(1)} %bitcast.101, bf16[4,512,128]{2,1,0:T(8,128)(2,1)S(1)} %get-tuple-element.168, s32[]{:T(128)S(6)} %copy.45), kind=kOutput, calls=%fused_computation.58.clone.1 | convolution fusion | flops 273678848 | bytes 5120004 | tf_op jit(solution)/shard_map/while/body/eval_jaxpr/sub | solution.py:80
  165.0 2.7 %fusion.64 = bf16[128,8,256]{2,0,1:T(8,128)(2,1)S(1)} fusion(f32[8,256,512]{1,2,0:T(8,128)} %get-tuple-element.145, f32[8,256]{1,0:T(8,128)S(1)} %get-tuple-element.146, bf16[4,512,128]{1,2,0:T(8,128)(2,1)} %get-tuple-element.167, s32[]{:T(128)S(6)} %copy.45), kind=kOutput, calls=%fused_computation.10.clone.1 | convolution fusion | flops 270794752 | bytes 4857860 | tf_op jit(solution)/shard_map/while/body/eval_jaxpr/qrs,sd->rqd/dot_general | solution.py:82
  167.7 0.9 constant_dynamic-update-slice_fusion.2
  168.6 0.2 fusion.62
  168.9 3.8 %fusion.63 = (f32[8,256]{1,0:T(8,128)S(1)}, f32[8,256,512]{1,2,0:T(8,128)}) fusion(pred[256,512]{0,1:T(8,128)(4,1)S(1)} %fusion.62, bf16[256,8,128]{0,2,1:T(8,128)(2,1)S(1)} %bitcast.101, bf16[4,512,128]{2,1,0:T(8,128)(2,1)S(1)} %get-tuple-element.168, s32[]{:T(128)S(6)} %copy.45), kind=kOutput, calls=%fused_computation.58.clone.1 | convolution fusion | flops 273678848 | bytes 5120004 | tf_op jit(solution)/shard_map/while/body/eval_jaxpr/sub | solution.py:80
  172.7 2.7 %fusion.64 = bf16[128,8,256]{2,0,1:T(8,128)(2,1)S(1)} fusion(f32[8,256,512]{1,2,0:T(8,128)} %get-tuple-element.145, f32[8,256]{1,0:T(8,128)S(1)} %get-tuple-element.146, bf16[4,512,128]{1,2,0:T(8,128)(2,1)} %get-tuple-element.167, s32[]{:T(128)S(6)} %copy.45), kind=kOutput, calls=%fused_computation.10.clone.1 | convolution fusion | flops 270794752 | bytes 4857860 | tf_op jit(solution)/shard_map/while/body/eval_jaxpr/qrs,sd->rqd/dot_general | solution.py:82
  175.4 0.9 constant_dynamic-update-slice_fusion.2
  176.2 0.2 fusion.62
  176.5 3.8 %fusion.63 = (f32[8,256]{1,0:T(8,128)S(1)}, f32[8,256,512]{1,2,0:T(8,128)}) fusion(pred[256,512]{0,1:T(8,128)(4,1)S(1)} %fusion.62, bf16[256,8,128]{0,2,1:T(8,128)(2,1)S(1)} %bitcast.101, bf16[4,512,128]{2,1,0:T(8,128)(2,1)S(1)} %get-tuple-element.168, s32[]{:T(128)S(6)} %copy.45), kind=kOutput, calls=%fused_computation.58.clone.1 | convolution fusion | flops 273678848 | bytes 5120004 | tf_op jit(solution)/shard_map/while/body/eval_jaxpr/sub | solution.py:80
  180.3 2.7 %fusion.64 = bf16[128,8,256]{2,0,1:T(8,128)(2,1)S(1)} fusion(f32[8,256,512]{1,2,0:T(8,128)} %get-tuple-element.145, f32[8,256]{1,0:T(8,128)S(1)} %get-tuple-element.146, bf16[4,512,128]{1,2,0:T(8,128)(2,1)} %get-tuple-element.167, s32[]{:T(128)S(6)} %copy.45), kind=kOutput, calls=%fused_computation.10.clone.1 | convolution fusion | flops 270794752 | bytes 4857860 | tf_op jit(solution)/shard_map/while/body/eval_jaxpr/qrs,sd->rqd/dot_general | solution.py:82
  183.0 0.9 constant_dynamic-update-slice_fusion.2
  183.9 0.2 fusion.62
  184.1 3.8 %fusion.63 = (f32[8,256]{1,0:T(8,128)S(1)}, f32[8,256,512]{1,2,0:T(8,128)}) fusion(pred[256,512]{0,1:T(8,128)(4,1)S(1)} %fusion.62, bf16[256,8,128]{0,2,1:T(8,128)(2,1)S(1)} %bitcast.101, bf16[4,512,128]{2,1,0:T(8,128)(2,1)S(1)} %get-tuple-element.168, s32[]{:T(128)S(6)} %copy.45), kind=kOutput, calls=%fused_computation.58.clone.1 | convolution fusion | flops 273678848 | bytes 5120004 | tf_op jit(solution)/shard_map/while/body/eval_jaxpr/sub | solution.py:80
  187.9 2.7 %fusion.64 = bf16[128,8,256]{2,0,1:T(8,128)(2,1)S(1)} fusion(f32[8,256,512]{1,2,0:T(8,128)} %get-tuple-element.145, f32[8,256]{1,0:T(8,128)S(1)} %get-tuple-element.146, bf16[4,512,128]{1,2,0:T(8,128)(2,1)} %get-tuple-element.167, s32[]{:T(128)S(6)} %copy.45), kind=kOutput, calls=%fused_computation.10.clone.1 | convolution fusion | flops 270794752 | bytes 4857860 | tf_op jit(solution)/shard_map/while/body/eval_jaxpr/qrs,sd->rqd/dot_general | solution.py:82
  190.6 0.8 constant_dynamic-update-slice_fusion.2
  191.5 5.1 %collective-permute-start.2 = (bf16[256,4096]{0,1:T(8,128)(2,1)}, bf16[256,4096]{0,1:T(8,128)(2,1)}, u32[]{:S(2)}, u32[]{:S(2)}) collective-permute-start(bf16[256,4096]{0,1:T(8,128)(2,1)} %bitcast.105), channel_id=1, source_target_pairs={{1,0},{2,1},{3,2},{4,3},{5,4},{6,5},{7,6},{8,7},{9,8},{10,9},{11,1... | collective-permute-start | bytes 6291464 | tf_op jit(solution)/shard_map/ppermute | solution.py:17
  196.6 0.0 collective-permute-start.1
  196.6 0.7 fusion.47
  199.1 0.6 compare_and_fusion.1
  199.7 0.1 broadcast_in_dim.159
  199.8 0.7 compare_and_fusion
  200.5 0.1 broadcast_in_dim.164
  200.6 0.7 compare_and_fusion.2
  201.3 0.1 broadcast_in_dim.153
  201.4 0.1 fusion.41
  201.5 0.1 select_reduce_fusion
  201.6 0.1 select_compare_fusion
  201.7 2.9 %copy.30 = bf16[256,4096]{1,0:T(8,128)(2,1)S(1)} copy(bf16[256,4096]{0,1:T(8,128)(2,1)} %bitcast.107) | data formatting | bytes 4194304 | tf_op jit(solution)/shard_map/reshape | solution.py:88
  204.6 36.0 %collective-permute-done.2 = bf16[256,4096]{0,1:T(8,128)(2,1)} collective-permute-done((bf16[256,4096]{0,1:T(8,128)(2,1)}, bf16[256,4096]{0,1:T(8,128)(2,1)}, u32[]{:S(2)}, u32[]{:S(2)}) %collective-permute-start.2) | collective-permute-done | bytes 2097184 | tf_op jit(solution)/shard_map/ppermute | solution.py:17
  240.6 4.2 %copy.31 = bf16[256,4096]{1,0:T(8,128)(2,1)} copy(bf16[256,4096]{0,1:T(8,128)(2,1)} %collective-permute-done.2) | data formatting | bytes 4194304 | tf_op jit(solution)/shard_map/ppermute | solution.py:17
  244.7 4.1 %copy.29 = bf16[256,4096]{1,0:T(8,128)(2,1)} copy(bf16[256,4096]{0,1:T(8,128)(2,1)} %collective-permute-done.1) | data formatting | bytes 4194304 | tf_op jit(solution)/shard_map/ppermute | solution.py:17
  248.9 5.3 %fusion.35 = bf16[512,4096]{1,0:T(8,128)(2,1)} fusion(pred[512]{0:T(512)(128)(4,1)S(1)} %broadcast_in_dim.165, pred[512]{0:T(512)(128)(4,1)S(1)} %broadcast_in_dim.160, pred[512]{0:T(512)(128)(4,1)S(1)} %broadcast_in_dim.154, pred[512]{0:T(512)(128)(4,1)S(1)} %ge.27, bf16[256,4096]{1,0:T(8,128)(2,1)} %copy.31, bf16[256,4096]{1,0:T(8,128)(2,1)S(1)} %copy.30, ...), kind=kLoop, calls=%fused_computation.32 | loop fusion | flops 8388608 | bytes 10487808 | tf_op jit(solution)/shard_map/jit(_where)/select_n | solution.py:131
  (21 shorter events, 0.3 us)
Async XLA Ops:
  6.5 134.1 %all-gather.2.cloned.1.call-start = ((), (), s32[]{:S(2)}) async-start(), calls=%async_computation | async-start | bytes 17825792 | tf_op jit(solution)/shard_map/all_gather | solution.py:109
  11.1 141.6 %copy-start = (s32[4096]{0:T(1024)S(1)}, s32[4096]{0:T(1024)}, u32[]{:S(2)}) copy-start(s32[4096]{0:T(1024)} %param.13) | copy-start | bytes 49156
  152.1 6.6 %collective-permute-start = (bf16[256,1024]{1,0:T(8,128)(2,1)S(1)}, bf16[256,1024]{1,0:T(8,128)(2,1)}, u32[]{:S(2)}, u32[]{:S(2)}) collective-permute-start(bf16[256,1024]{1,0:T(8,128)(2,1)S(1)} %fusion.36), channel_id=1, source_target_pairs={{15,0},{0,1},{1,2},{2,3},{3,4},{4,5},{5,6},{6,7},{7,8},{8,9},{9,10... | collective-permute-start | bytes 1572872 | tf_op jit(solution)/shard_map/ppermute | solution.py:17
  161.0 35.6 %copy-start.1 = (s32[16]{0:T(128)S(1)}, s32[16]{0:T(128)}, u32[]{:S(2)}) copy-start(s32[16]{0:T(128)} %param.15) | copy-start | bytes 196
  161.0 35.6 %copy-start.2 = (s32[16]{0:T(128)S(1)}, s32[16]{0:T(128)}, u32[]{:S(2)}) copy-start(s32[16]{0:T(128)} %param.14) | copy-start | bytes 196
  191.5 49.1 %collective-permute-start.2 = (bf16[256,4096]{0,1:T(8,128)(2,1)}, bf16[256,4096]{0,1:T(8,128)(2,1)}, u32[]{:S(2)}, u32[]{:S(2)}) collective-permute-start(bf16[256,4096]{0,1:T(8,128)(2,1)} %bitcast.105), channel_id=1, source_target_pairs={{1,0},{2,1},{3,2},{4,3},{5,4},{6,5},{7,6},{8,7},{9,8},{10,9},{11,1... | collective-permute-start | bytes 6291464 | tf_op jit(solution)/shard_map/ppermute | solution.py:17
  196.6 48.1 %collective-permute-start.1 = (bf16[256,4096]{0,1:T(8,128)(2,1)}, bf16[256,4096]{0,1:T(8,128)(2,1)}, u32[]{:S(2)}, u32[]{:S(2)}) collective-permute-start(bf16[256,4096]{0,1:T(8,128)(2,1)} %bitcast.106), channel_id=1, source_target_pairs={{15,0},{0,1},{1,2},{2,3},{3,4},{4,5},{5,6},{6,7},{7,8},{8,9},{9,10... | collective-permute-start | bytes 6291464 | tf_op jit(solution)/shard_map/ppermute | solution.py:17
Sparse Core Ops, SparseCore 0:
  11.2 129.3 all-gather.1
where the time goes:
time: 262 us; the launch traced here: 261 us
  waiting for transfers between devices  168 us (64%)
  matrix products  37.6 us (14%)
  local copies, waits for them, and re-layouts  21.9 us (8%)
  between operations  15.3 us (6%)
  other arithmetic  12.2 us (5%)
  starting transfers between devices  5.59 us (2%)
    all_gather x1, waiting for transfers between devices, per_device(): lax.all_gather(local_weights, 'shard', axis=0, tiled=True)  130 us
    ppermute x3, waiting for transfers between devices, passed_along(): return lax.ppermute(block, axis, route)  38.7 us
    sub x4, matrix products, one_group(): raised = jnp.where(allowed[None], jnp.exp(masked - row_max), 0.0)  15.1 us
    dot_general x1, matrix products, projector(): return jnp.dot(hidden_rows, portion, preferred_element_type=jnp.float32)  11.5 us
    dot_general x4, matrix products, one_group(): jnp.einsum('qrs,sd->rqd', weights, value_group, preferred_element_type=jn...  10.9 us
    ppermute x2, local copies, waits for them, and re-layouts, passed_along(): return lax.ppermute(block, axis, route)  8.29 us
    ppermute x3, starting transfers between devices, passed_along(): return lax.ppermute(block, axis, route)  5.59 us
    select_n x1, other arithmetic, per_device(): jnp.where(slot_segment[:, None] >= 0, attended, jnp.zeros_like(attended))  5.25 us
  transfers between devices with their start and end apart: 4, of which 3 were waited for; matrix products, arithmetic and copies ran while one was open for 5% of the time, Pallas kernels for 0%

commit v1 on v0

v1 whole, which is shorter than its diff:
```python
import jax
import jax.numpy as jnp
from jax import lax
from jax.experimental import pallas as pl
from jax.experimental.pallas import tpu as pltpu
from jax.sharding import PartitionSpec as P

KVH = 4
HD = 128
QPK = 8
QB = 128
CAP = 2
HOP = 1
LOG2E = 1.4426950408889634


def passed_along(block, axis, distance):
    devices = range(lax.axis_size(axis))
    route = [((i - distance) % len(devices), i) for i in devices]
    return lax.ppermute(block, axis, route)


def dequantize(codes, scales):
    row_count, col_count = codes.shape
    blocks = codes.astype(jnp.float32).reshape(row_count // QB, QB, col_count // QB, QB)
    scaled = blocks * scales[:, None, :, None]
    return scaled.reshape(row_count, col_count).astype(jnp.bfloat16)


def regroup(payload, target_device, target_slot):
    cycle_size = lax.axis_size("shard")
    own_index = lax.axis_index("shard")
    slot_ids = jnp.arange(CAP, dtype=jnp.int32)
    result = jnp.zeros((CAP,) + payload.shape, payload.dtype)
    for offset in range(-HOP, HOP + 1):
        if offset == 0:
            arrived = payload
        else:
            arrived = passed_along(payload, "shard", offset)
        source = (own_index - offset) % cycle_size
        landing = lax.dynamic_index_in_dim(target_device, source, keepdims=False) == own_index
        wanted = lax.dynamic_index_in_dim(target_slot, source, keepdims=False)
        chosen = jnp.logical_and(slot_ids == wanted, landing)
        result = jnp.where(chosen[:, None, None], arrived[None], result)
    return result.reshape(CAP * payload.shape[0], payload.shape[1])


def slot_segments(segment, target_device, target_slot):
    own_index = lax.axis_index("shard")
    block_count = target_device.shape[0]
    segment_rows = segment.reshape(block_count, -1)
    matches = jnp.logical_and(
        target_device[:, None] == own_index,
        target_slot[:, None] == jnp.arange(CAP, dtype=jnp.int32)[None, :],
    )
    summed = jnp.sum(jnp.where(matches[:, :, None], segment_rows[:, None, :], 0), axis=0)
    present = jnp.any(matches, axis=0)
    return jnp.where(present[:, None], summed, -1).reshape(-1)


def projector(hidden_rows, portion):
    return jnp.dot(hidden_rows, portion, preferred_element_type=jnp.float32)


def attention_kernel(row_seg_ref, col_seg_ref, q_ref, k_ref, v_ref, out_ref, bias_ref):
    rows = q_ref.shape[0]
    half = rows // CAP
    factor = HD ** (-0.5) * LOG2E

    @pl.when(pl.program_id(0) == 0)
    def _():
        row_index = lax.broadcasted_iota(jnp.int32, (rows, rows), 0)
        col_index = lax.broadcasted_iota(jnp.int32, (rows, rows), 1)
        allowed = jnp.logical_and(row_seg_ref[...] == col_seg_ref[...], col_index <= row_index)
        bias_ref[...] = jnp.where(allowed, 0.0, -1e30)

    ones = jnp.ones((rows, HD), jnp.bfloat16)
    v_wide = jnp.concatenate([v_ref[...], ones], axis=1)
    for slot in range(CAP):
        reach = (slot + 1) * half
        span = slice(slot * half, reach)
        keys = k_ref[:reach, :]
        present = row_seg_ref[span, :] >= 0
        for head in range(QPK):
            cols = slice(head * HD, (head + 1) * HD)
            scores = lax.dot_general(
                q_ref[span, cols], keys, (((1,), (1,)), ((), ())),
                preferred_element_type=jnp.float32,
            )
            scores = scores + bias_ref[span, :reach]
            top = jnp.max(scores, axis=1, keepdims=True)
            raised = jnp.exp2((scores - top) * factor).astype(jnp.bfloat16)
            mixed = jnp.dot(raised, v_wide[:reach], preferred_element_type=jnp.float32)
            result = mixed[:, :HD] / mixed[:, HD:]
            out_ref[span, cols] = jnp.where(present, result, 0.0).astype(jnp.bfloat16)


def attend(slot_queries, slot_kv, slot_segment):
    rows = slot_queries.shape[0]
    width = QPK * HD
    return pl.pallas_call(
        attention_kernel,
        out_shape=jax.ShapeDtypeStruct(slot_queries.shape, jnp.bfloat16),
        grid=(KVH,),
        in_specs=[
            pl.BlockSpec((rows, 1), lambda g: (0, 0)),
            pl.BlockSpec((1, rows), lambda g: (0, 0)),
            pl.BlockSpec((rows, width), lambda g: (0, g)),
            pl.BlockSpec((rows, HD), lambda g: (0, g)),
            pl.BlockSpec((rows, HD), lambda g: (0, KVH + g)),
        ],
        out_specs=pl.BlockSpec((rows, width), lambda g: (0, g)),
        scratch_shapes=[pltpu.VMEM((rows, rows), jnp.float32)],
        compiler_params=pltpu.CompilerParams(vmem_limit_bytes=32 * 1024 * 1024),
    )(slot_segment[:, None], slot_segment[None, :], slot_queries, slot_kv, slot_kv)


def per_device(
    hidden,
    queries,
    segment,
    target_device,
    target_slot,
    key_codes,
    key_scales,
    value_codes,
    value_scales,
):
    local_weights = jnp.concatenate(
        (dequantize(key_codes, key_scales), dequantize(value_codes, value_scales)), axis=1
    )
    depth = local_weights.shape[0]
    block_rows = hidden.shape[0]
    cycle_size = lax.axis_size("shard")
    core = lax.axis_index("shard") % 2
    pairs = [(i, i ^ 1) for i in range(cycle_size)]
    same_core = [list(range(c, cycle_size, 2)) for c in range(2)]
    weights = lax.all_gather(
        local_weights, "shard", axis=0, tiled=True, axis_index_groups=same_core
    )
    columns = hidden.reshape(block_rows, cycle_size // 2, 2, depth)
    kept = lax.dynamic_index_in_dim(columns, core, 2, keepdims=False).reshape(block_rows, -1)
    given = lax.dynamic_index_in_dim(columns, 1 - core, 2, keepdims=False).reshape(block_rows, -1)
    taken = lax.ppermute(given, "shard", pairs)
    slot_segment = slot_segments(segment, target_device, target_slot)
    slot_queries = regroup(queries, target_device, target_slot)
    partial = projector(jnp.concatenate((kept, taken), axis=0), weights)
    other = lax.ppermute(partial[block_rows:], "shard", pairs)
    key_value = (partial[:block_rows] + other).astype(jnp.bfloat16)
    slot_kv = regroup(key_value, target_device, target_slot)
    return attend(slot_queries, slot_kv, slot_segment)


def solution(mesh):
    return jax.shard_map(
        per_device,
        mesh=mesh,
        in_specs=(
            P(("groups", "shard"), None),
            P(("groups", "shard"), None),
            P("groups"),
            P("groups"),
            P("groups"),
            P("shard", None),
            P("shard", None),
            P("shard", None),
            P("shard", None),
        ),
        out_specs=P(("groups", "shard"), None),
        check_vma=False,
    )
```

time: 262 us -> 208 us (0.79)
  matrix products: 37.6 us -> 7.61 us
  waiting for transfers between devices: 168 us -> 147 us
  Pallas kernels: 0 us -> 11.5 us
  local copies, waits for them, and re-layouts: 21.9 us -> 13.3 us
  other arithmetic: 12.2 us -> 8.73 us
    ppermute x3 -> x4, waiting for transfers between devices: 38.7 us -> 10.3 us  [passed_along(): return lax.ppermute(block, axis, route)]
    sub x4 -> x0, matrix products: 15.1 us -> none  [one_group(): raised = jnp.where(allowed[None], jnp.exp(masked - row_max), 0.0)]
    pallas_call x0 -> x1, Pallas kernels: none -> 11.5 us  [attend(): pl.pallas_call(attention_kernel, out_shape=jax.ShapeDtypeStruct(slot_quer...]
    dot_general x4 -> x0, matrix products: 10.9 us -> none  [one_group(): jnp.einsum('qrs,sd->rqd', weights, value_group, preferred_element_type=jn...]
    ppermute x2 -> x0, local copies, waits for them, and re-layouts: 8.29 us -> none  [passed_along(): return lax.ppermute(block, axis, route)]
    unnamed x7 -> x15, local copies, waits for them, and re-layouts: 3.29 us -> 7.86 us
    reshape x3 -> x0, local copies, waits for them, and re-layouts: 4.01 us -> none  [the longest x1 2.91 us: attend(): return outputs.transpose(1, 0, 2).reshape(query_count, KVH * head_width)]
    ppermute x0 -> x2, waiting for transfers between devices: none -> 3.92 us  [the longest x1 3.92 us: per_device(): taken = lax.ppermute(given, 'shard', pairs)]
  transfers between devices with their start and end apart: 4 -> 7, of which waited for: 3 -> 4; matrix products, arithmetic and copies ran while one was open for 5% -> 12% of each run, Pallas kernels for 0% -> 0%
where the time goes in v1:
time: 208 us
  waiting for transfers between devices  147 us (71%)
  between operations  15.5 us (7%)
  local copies, waits for them, and re-layouts  13.3 us (6%)
  Pallas kernels  11.5 us (6%)
  other arithmetic  8.73 us (4%)
  matrix products  7.61 us (4%)
  starting transfers between devices  4.64 us (2%)
    all_gather x1, waiting for transfers between devices, per_device(): lax.all_gather(local_weights, 'shard', axis=0, tiled=True, axis_index_gro...  133 us
    pallas_call x1, Pallas kernels, attend(): pl.pallas_call(attention_kernel, out_shape=jax.ShapeDtypeStruct(slot_quer...  11.5 us
    ppermute x4, waiting for transfers between devices, passed_along(): return lax.ppermute(block, axis, route)  10.3 us
    unnamed x15, local copies, waits for them, and re-layouts  7.86 us
    dot_general x1, matrix products, projector(): return jnp.dot(hidden_rows, portion, preferred_element_type=jnp.float32)  7.61 us
  transfers between devices with their start and end apart: 7, of which 4 were waited for; matrix products, arithmetic and copies ran while one was open for 12% of the time, Pallas kernels for 0%

profile of v1, /device:TPU:1, one launch (start us, length us, event | category | flops | bytes accessed | tf_op | source)
XLA Modules:
  0.0 208.0 jit_solution(7979440737980033470)
XLA Ops:
  6.5 0.0 copy-start.2
  6.5 0.0 copy-start.1
  6.5 0.0 all-gather.2.cloned.1.call-start
  6.5 1.0 mul.22
  7.5 0.9 mul.25
  8.4 0.0 copy-done.2
  8.4 0.0 copy-done.1
  8.4 0.4 fusion.6
  8.8 1.1 pad_maximum_fusion
  10.0 0.0 all-gather.2.cloned.1.call-update
  10.0 6.4 %copy.13 = bf16[256,8192]{0,1:T(8,128)(2,1)} copy(bf16[256,8192]{1,0:T(8,128)(2,1)} %param.9) | data formatting | bytes 8388608 | tf_op args[0]
  16.4 2.5 %constant_dynamic-slice_fusion = (bf16[256,8,1,512]{0,3,2,1:T(8,128)(2,1)S(1)}, bf16[256,8,1,512]{0,3,2,1:T(8,128)(2,1)S(1)}) fusion(bf16[256,8,2,512]{0,3,2,1:T(8,128)(2,1)} %bitcast.53, s32[]{:T(128)S(6)} %select_n.119, s32[]{:T(128)S(6)} %select_n.120), kind=kLoop, calls=%fused_computation.23 | loop fusion | bytes 8388616 | tf_op jit(solution)/shard_map/jit(dynamic_index_in_dim)/dynamic_slice | solution.py:142
  18.9 0.1 collective-permute-start.2
  19.0 2.6 %collective-permute-start = (bf16[256,4096]{1,0:T(8,128)(2,1)}, bf16[256,4096]{1,0:T(8,128)(2,1)}, u32[]{:S(2)}, u32[]{:S(2)}) collective-permute-start(bf16[256,4096]{1,0:T(8,128)(2,1)} %param.10), channel_id=1, source_target_pairs={{15,0},{0,1},{1,2},{2,3},{3,4},{4,5},{5,6},{6,7},{7,8},{8,9},{9,10... | collective-permute-start | bytes 6291464 | tf_op jit(solution)/shard_map/ppermute | solution.py:20
  21.7 0.0 collective-permute-start.1
  21.7 3.9 %collective-permute-done.2 = bf16[256,4096]{0,1:T(8,128)(2,1)} collective-permute-done((bf16[256,4096]{0,1:T(8,128)(2,1)S(1)}, bf16[256,4096]{0,1:T(8,128)(2,1)}, u32[]{:S(2)}, u32[]{:S(2)}) %collective-permute-start.2) | collective-permute-done | bytes 2097184 | tf_op jit(solution)/shard_map/ppermute | solution.py:144
  25.6 132.5 %all-gather.2.cloned.1.call-done = bf16[4096,1024]{1,0:T(8,128)(2,1)} async-done(((bf16[512,1024]{1,0:T(8,128)(2,1)}), bf16[4096,1024]{1,0:T(8,128)(2,1)}) %all-gather.2.cloned.1.call-update) | async-done | bytes 8388624 | tf_op jit(solution)/shard_map/all_gather | solution.py:138
  158.1 7.6 %fusion = f32[512,1024]{1,0:T(8,128)S(1)} fusion(bf16[4096,1024]{1,0:T(8,128)(2,1)} %all-gather.2.cloned.1.call-done, bf16[256,4096]{0,1:T(8,128)(2,1)} %collective-permute-done.2, bf16[256,4096]{0,1:T(8,128)(2,1)S(1)} %bitcast.56), kind=kOutput, calls=%fused_computation | convolution fusion | flops 4303355904 | bytes 14680064 | tf_op jit(solution)/shard_map/dot_general | solution.py:62
  165.7 0.0 copy-start
  165.7 1.3 copy-done
  167.1 0.0 copy-start.4
  167.1 0.1 slice.9
  167.1 1.1 collective-permute-start.3
  168.3 0.0 copy-done.4
  168.3 0.0 copy-done.5
  168.3 0.7 fusion.13
  169.7 0.6 compare_and_fusion.2
  170.2 0.1 broadcast_in_dim.161
  171.0 0.6 compare_and_fusion.1
  171.6 0.1 broadcast_in_dim.166
  172.2 0.6 compare_and_fusion
  172.9 0.1 broadcast_in_dim.171
  173.0 0.0 copy-done.3
  173.0 0.0 collective-permute-done.3
  173.0 1.4 fusion.8
  174.4 0.7 collective-permute-start.4
  175.1 0.0 collective-permute-start.5
  175.1 0.1 fusion.12
  175.2 0.1 select_reduce_fusion
  175.3 0.1 select_bitcast_fusion
  175.4 0.1 copy.16
  175.6 0.0 collective-permute-done
  175.6 0.0 collective-permute-done.1
  175.6 3.4 %fusion.5.q_ref = bf16[512,4096]{1,0:T(8,128)(2,1)S(1)} fusion(pred[512]{0:T(512)(128)(4,1)S(1)} %broadcast_in_dim.172, pred[512]{0:T(512)(128)(4,1)S(1)} %broadcast_in_dim.167, pred[512]{0:T(512)(128)(4,1)S(1)} %broadcast_in_dim.162, bf16[256,4096]{1,0:T(8,128)(2,1)} %collective-permute-done.1, bf16[256,4096]{1,0:T(8,128)(2,1)} %param.10, ...), kind=kLoop, calls=%fused_computation.6 | loop fusion | flops 6291456 | bytes 10487296 | tf_op jit(solution)/shard_map/jit(_where)/select_n | solution.py:44
  179.0 7.9 %collective-permute-done.4 = bf16[256,1024]{1,0:T(8,128)(2,1)S(1)} collective-permute-done((bf16[256,1024]{1,0:T(8,128)(2,1)S(1)}, bf16[256,1024]{1,0:T(8,128)(2,1)S(1)}, u32[]{:S(2)}, u32[]{:S(2)}) %collective-permute-start.4) | collective-permute-done | bytes 524320 | tf_op jit(solution)/shard_map/ppermute | solution.py:20
  186.9 2.5 %collective-permute-done.5 = bf16[256,1024]{1,0:T(8,128)(2,1)S(1)} collective-permute-done((bf16[256,1024]{1,0:T(8,128)(2,1)S(1)}, bf16[256,1024]{1,0:T(8,128)(2,1)S(1)}, u32[]{:S(2)}, u32[]{:S(2)}) %collective-permute-start.5) | collective-permute-done | bytes 524320 | tf_op jit(solution)/shard_map/ppermute | solution.py:20
  189.4 0.3 fusion.10.k_ref.v_ref
  189.7 11.5 %shard_map.91 = bf16[512,4096]{1,0:T(8,128)(2,1)} custom-call(s32[512,1]{1,0:T(8,128)S(1)} %bitcast.50, s32[1,512]{1,0:T(1,128)S(1)} %bitcast.52, bf16[512,4096]{1,0:T(8,128)(2,1)S(1)} %fusion.5.q_ref, bf16[512,1024]{1,0:T(8,128)(2,1)S(1)} %fusion.10.k_ref.v_ref, bf16[512,1024]{1,0:T(8,128)(2,1)S(1)} %fusion.10.k_ref.v_ref), custom_call_target="tpu_custom_call" | custom-call | tf_op jit(solution)/shard_map/pallas_call | solution.py:101
  (8 shorter events, 0.1 us)
Async XLA Ops:
  6.5 1.9 copy-start.2
  6.5 1.9 copy-start.1
  6.5 151.6 %all-gather.2.cloned.1.call-start = ((), (), s32[]{:S(2)}) async-start(), calls=%async_computation | async-start | bytes 9437184 | tf_op jit(solution)/shard_map/all_gather | solution.py:138
  18.9 6.7 %collective-permute-start.2 = (bf16[256,4096]{0,1:T(8,128)(2,1)S(1)}, bf16[256,4096]{0,1:T(8,128)(2,1)}, u32[]{:S(2)}, u32[]{:S(2)}) collective-permute-start(bf16[256,4096]{0,1:T(8,128)(2,1)S(1)} %bitcast.57), channel_id=1, source_target_pairs={{0,1},{1,0},{2,3},{3,2},{4,5},{5,4},{6,7},{7,6},{8,9},{9,8},{10,11... | collective-permute-start | bytes 6291464 | tf_op jit(solution)/shard_map/ppermute | solution.py:144
  19.0 156.5 %collective-permute-start = (bf16[256,4096]{1,0:T(8,128)(2,1)}, bf16[256,4096]{1,0:T(8,128)(2,1)}, u32[]{:S(2)}, u32[]{:S(2)}) collective-permute-start(bf16[256,4096]{1,0:T(8,128)(2,1)} %param.10), channel_id=1, source_target_pairs={{15,0},{0,1},{1,2},{2,3},{3,4},{4,5},{5,6},{6,7},{7,8},{8,9},{9,10... | collective-permute-start | bytes 6291464 | tf_op jit(solution)/shard_map/ppermute | solution.py:20
  21.7 153.9 %collective-permute-start.1 = (bf16[256,4096]{1,0:T(8,128)(2,1)}, bf16[256,4096]{1,0:T(8,128)(2,1)}, u32[]{:S(2)}, u32[]{:S(2)}) collective-permute-start(bf16[256,4096]{1,0:T(8,128)(2,1)} %param.10), channel_id=1, source_target_pairs={{1,0},{2,1},{3,2},{4,3},{5,4},{6,5},{7,6},{8,7},{9,8},{10,9},{11,1... | collective-permute-start | bytes 6291464 | tf_op jit(solution)/shard_map/ppermute | solution.py:20
  165.7 1.3 copy-start
  167.1 1.2 copy-start.4
  167.1 1.2 copy-start.5
  167.1 5.9 %copy-start.3 = (s32[4096]{0:T(1024)S(1)}, s32[4096]{0:T(1024)}, u32[]{:S(2)}) copy-start(s32[4096]{0:T(1024)} %param.11) | copy-start | bytes 49156
  167.1 5.9 %collective-permute-start.3 = (f32[256,1024]{1,0:T(8,128)S(1)}, f32[256,1024]{1,0:T(8,128)S(1)}, u32[]{:S(2)}, u32[]{:S(2)}) collective-permute-start(f32[256,1024]{1,0:T(8,128)S(1)} %slice.9), channel_id=1, source_target_pairs={{0,1},{1,0},{2,3},{3,2},{4,5},{5,4},{6,7},{7,6},{8,9},{9,8},{10,11... | collective-permute-start | bytes 3145736 | tf_op jit(solution)/shard_map/ppermute | solution.py:148
  174.4 12.5 %collective-permute-start.4 = (bf16[256,1024]{1,0:T(8,128)(2,1)S(1)}, bf16[256,1024]{1,0:T(8,128)(2,1)S(1)}, u32[]{:S(2)}, u32[]{:S(2)}) collective-permute-start(bf16[256,1024]{1,0:T(8,128)(2,1)S(1)} %fusion.8), channel_id=1, source_target_pairs={{15,0},{0,1},{1,2},{2,3},{3,4},{4,5},{5,6},{6,7},{7,8},{8,9},{9,10... | collective-permute-start | bytes 1572872 | tf_op jit(solution)/shard_map/ppermute | solution.py:20
  175.1 14.2 %collective-permute-start.5 = (bf16[256,1024]{1,0:T(8,128)(2,1)S(1)}, bf16[256,1024]{1,0:T(8,128)(2,1)S(1)}, u32[]{:S(2)}, u32[]{:S(2)}) collective-permute-start(bf16[256,1024]{1,0:T(8,128)(2,1)S(1)} %fusion.8), channel_id=1, source_target_pairs={{1,0},{2,1},{3,2},{4,3},{5,4},{6,5},{7,6},{8,7},{9,8},{10,9},{11,1... | collective-permute-start | bytes 1572872 | tf_op jit(solution)/shard_map/ppermute | solution.py:20
Sparse Core Ops, SparseCore 0:
  10.1 147.9 all-gather.1

commit v2 on v1

v2 whole, which is shorter than its diff:
```python
import functools

import jax
import jax.numpy as jnp
from jax import lax
from jax.experimental import pallas as pl
from jax.experimental.pallas import tpu as pltpu
from jax.sharding import PartitionSpec as P

KVH = 4
HD = 128
QPK = 8
QB = 128
CAP = 2
HOP = 1
TILE = 256
MESH = pl.DeviceIdType.MESH
LOG2E = 1.4426950408889634


def slot_segments(segment, target_device, target_slot):
    own_index = lax.axis_index("shard")
    block_count = target_device.shape[0]
    segment_rows = segment.reshape(block_count, -1)
    matches = jnp.logical_and(
        target_device[:, None] == own_index,
        target_slot[:, None] == jnp.arange(CAP, dtype=jnp.int32)[None, :],
    )
    summed = jnp.sum(jnp.where(matches[:, :, None], segment_rows[:, None, :], 0), axis=0)
    present = jnp.any(matches, axis=0)
    return jnp.where(present[:, None], summed, -1).reshape(-1)


def ring_chip(place, chips, snake):
    if not snake:
        return place
    turned = place // (chips // 2)
    level = (1 - turned) * place + turned * (chips - 1 - place)
    return 2 * level + turned


def ring_place(chip, chips, snake):
    if not snake:
        return chip
    level, side = chip // 2, chip % 2
    return (1 - side) * level + side * (chips - 1 - level)


def row_parts(start, count):
    first = (count // 2 + 15) // 16 * 16
    return ((start, first), (start + first, count - first))


def gather_kernel(
    chips, snake,
    hidden_ref, queries_ref, key_codes_ref, value_codes_ref, key_scales_ref, value_scales_ref,
    q3_ref, kv3_ref,
    weights, rows_in, total, half_in, kv,
    own_sem, give_send, take_sem, up_send, up_recv, down_send, down_recv, x_send, x_recv,
    half_send, half_recv, move_send, move_recv, keep_sem,
):
    block_rows = hidden_ref.shape[0]
    depth, key_width = key_codes_ref.shape
    third = (depth // 3 + 8) // 16 * 16
    shards = 2 * chips
    group = lax.axis_index("groups")
    shard = lax.axis_index("shard")
    chip, core = shard // 2, shard % 2
    place = ring_place(chip, chips, snake)
    x_side = group % 2

    def ids(group_id, shard_id):
        return {"groups": group_id, "shard": shard_id}

    def on_ring(offset):
        return ring_chip((place + offset + chips) % chips, chips, snake)

    up = ids(group, on_ring(1) * 2 + core)
    down = ids(group, on_ring(-1) * 2 + core)
    across = ids(group + 1 - 2 * x_side, shard)
    sibling = ids(group, chip * 2 + 1 - core)
    right = ids(group, (shard + 1) % shards)
    left = ids(group, (shard + shards - 1) % shards)

    def remote(src, dst, send, recv, device):
        return pltpu.make_async_remote_copy(
            src_ref=src, dst_ref=dst, send_sem=send, recv_sem=recv,
            device_id=device, device_id_type=MESH,
        )

    barrier = pltpu.get_barrier_semaphore()
    for device in (up, down, across, right, left):
        pl.semaphore_signal(barrier, inc=1, device_id=device, device_id_type=MESH)

    local = []
    for m in range(chips):
        columns = pl.ds(pl.multiple_of((2 * m + core) * depth, 128), depth)
        local.append(pltpu.make_async_copy(
            hidden_ref.at[:, columns], rows_in.at[m, pl.ds(0, block_rows)], own_sem.at[m]
        ))
        local[-1].start()
    keep_q = pltpu.make_async_copy(queries_ref, q3_ref.at[0], keep_sem.at[0])
    keep_q.start()

    for codes_ref, scales_ref, base in (
        (key_codes_ref, key_scales_ref, 0), (value_codes_ref, value_scales_ref, key_width)
    ):
        for i in range(depth // QB):
            for j in range(key_width // QB):
                block = codes_ref[i * QB:(i + 1) * QB, j * QB:(j + 1) * QB].astype(jnp.float32)
                weights[chip, i * QB:(i + 1) * QB, base + j * QB:base + (j + 1) * QB] = (
                    block * scales_ref[i, j]
                ).astype(jnp.bfloat16)

    pl.semaphore_wait(barrier, 5)

    mine = row_parts(x_side * (depth - third), third)
    theirs = row_parts((1 - x_side) * (depth - third), third)
    shared = row_parts(third, depth - 2 * third)

    def piece(owner, part):
        return weights.at[owner, pl.ds(pl.multiple_of(part[0], 16), part[1])]

    sends = []

    def pass_up(step, sub, owner):
        ref = piece(owner, mine[sub])
        copy = remote(ref, ref, up_send.at[step, sub], up_recv.at[step, sub], up)
        copy.start()
        sends.append(copy)

    def pass_down(step, sub, owner):
        ref = piece(owner, shared[sub])
        copy = remote(ref, ref, down_send.at[step, sub], down_recv.at[step, sub], down)
        copy.start()
        sends.append(copy)

    def pass_across(step, sub, owner):
        ref = piece(owner, mine[sub])
        copy = remote(ref, ref, x_send.at[step, sub], x_recv.at[step, sub], across)
        copy.start()
        sends.append(copy)

    for sub in range(2):
        pass_up(0, sub, chip)
        pass_down(0, sub, chip)

    given = []
    for m in range(chips):
        columns = pl.ds(pl.multiple_of((2 * m + 1 - core) * depth, 128), depth)
        given.append(remote(
            hidden_ref.at[:, columns], rows_in.at[m, pl.ds(block_rows, block_rows)],
            give_send.at[m], take_sem.at[m], sibling,
        ))
        given[-1].start()

    moves = [
        remote(queries_ref, q3_ref.at[1], move_send.at[0], move_recv.at[0], right),
        remote(queries_ref, q3_ref.at[2], move_send.at[1], move_recv.at[1], left),
    ]
    for move in moves:
        move.start()

    def multiply(owner, first):
        @pl.loop(0, 2 * key_width // TILE)
        def _(t):
            columns = pl.ds(pl.multiple_of(t * TILE, TILE), TILE)
            product = jnp.dot(
                rows_in[owner], weights[owner, :, columns], preferred_element_type=jnp.float32
            )
            if first:
                total[:, columns] = product
            else:
                total[:, columns] += product

    def finish(back):
        owner = on_ring(-back)
        for sub in range(2):
            ref = piece(owner, theirs[sub])
            remote(
                ref, ref, x_send.at[back - 1, sub], x_recv.at[back - 1, sub], across
            ).wait_recv()
        multiply(owner, False)

    for step in range(1, chips):
        behind, ahead = on_ring(-step), on_ring(step)
        for sub in range(2):
            ref = piece(behind, mine[sub])
            remote(
                ref, ref, up_send.at[step - 1, sub], up_recv.at[step - 1, sub], up
            ).wait_recv()
            if step < chips - 1:
                pass_up(step, sub, behind)
            pass_across(step - 1, sub, behind)
            ref = piece(ahead, shared[sub])
            remote(
                ref, ref, down_send.at[step - 1, sub], down_recv.at[step - 1, sub], down
            ).wait_recv()
            if step < chips - 1:
                pass_down(step, sub, ahead)
        if step == 1:
            for m in range(chips):
                local[m].wait()
                given[m].wait()
            multiply(chip, True)
        for back in range(1, chips):
            if max(back, chips - back) == step - 1:
                finish(back)
    for back in range(1, chips):
        if max(back, chips - back) == chips - 1:
            finish(back)

    half = remote(
        total.at[pl.ds(block_rows, block_rows)], half_in, half_send, half_recv, sibling
    )
    half.start()
    half.wait()
    kv[...] = (total[:block_rows] + half_in[...]).astype(jnp.bfloat16)
    moves.append(remote(kv, kv3_ref.at[1], move_send.at[2], move_recv.at[2], right))
    moves.append(remote(kv, kv3_ref.at[2], move_send.at[3], move_recv.at[3], left))
    for move in moves[2:]:
        move.start()
    keep_kv = pltpu.make_async_copy(kv, kv3_ref.at[0], keep_sem.at[1])
    keep_kv.start()
    for copy in sends:
        copy.wait_send()
    for move in moves:
        move.wait()
    keep_q.wait()
    keep_kv.wait()


def gather_project(mesh_shape, hidden, queries, key_codes, key_scales, value_codes, value_scales):
    block_rows = hidden.shape[0]
    depth, key_width = key_codes.shape
    chips = mesh_shape["shard"] // 2
    snake = mesh_shape["groups"] == 2
    dma = pltpu.SemaphoreType.DMA
    any_space = pl.BlockSpec(memory_space=pl.ANY)
    vmem = pl.BlockSpec(memory_space=pltpu.VMEM)
    smem = pl.BlockSpec(memory_space=pltpu.SMEM)
    steps = (chips - 1, 2)
    return pl.pallas_call(
        functools.partial(gather_kernel, chips, snake),
        out_shape=(
            jax.ShapeDtypeStruct((3,) + queries.shape, jnp.bfloat16),
            jax.ShapeDtypeStruct((3, block_rows, 2 * key_width), jnp.bfloat16),
        ),
        in_specs=[any_space, any_space, vmem, vmem, smem, smem],
        out_specs=(any_space, any_space),
        scratch_shapes=[
            pltpu.VMEM((chips, depth, 2 * key_width), jnp.bfloat16),
            pltpu.VMEM((chips, 2 * block_rows, depth), jnp.bfloat16),
            pltpu.VMEM((2 * block_rows, 2 * key_width), jnp.float32),
            pltpu.VMEM((block_rows, 2 * key_width), jnp.float32),
            pltpu.VMEM((block_rows, 2 * key_width), jnp.bfloat16),
            dma((chips,)), dma((chips,)), dma((chips,)),
            dma(steps), dma(steps), dma(steps), dma(steps), dma(steps), dma(steps),
            dma, dma, dma((4,)), dma((4,)), dma((2,)),
        ],
        compiler_params=pltpu.CompilerParams(
            collective_id=0, has_side_effects=True, vmem_limit_bytes=40 * 1024 * 1024
        ),
        cost_estimate=pl.CostEstimate(
            flops=4 * block_rows * chips * depth * 2 * key_width,
            bytes_accessed=32 * 1024 * 1024, transcendentals=0,
        ),
    )(hidden, queries, key_codes, value_codes, key_scales, value_scales)


def attention_kernel(
    source_ref, row_seg_ref, col_seg_ref, q0_ref, q1_ref, k0_ref, k1_ref, v0_ref, v1_ref,
    out_ref, bias_ref,
):
    half = q0_ref.shape[1]
    rows = CAP * half
    factor = HD ** (-0.5) * LOG2E

    @pl.when(pl.program_id(0) == 0)
    def _():
        row_index = lax.broadcasted_iota(jnp.int32, (rows, rows), 0)
        col_index = lax.broadcasted_iota(jnp.int32, (rows, rows), 1)
        allowed = jnp.logical_and(row_seg_ref[...] == col_seg_ref[...], col_index <= row_index)
        bias_ref[...] = jnp.where(allowed, 0.0, -1e30)

    ones = jnp.ones((rows, HD), jnp.bfloat16)
    all_keys = jnp.concatenate([k0_ref[0], k1_ref[0]], axis=0)
    v_wide = jnp.concatenate(
        [jnp.concatenate([v0_ref[0], v1_ref[0]], axis=0), ones], axis=1
    )
    for slot, q_ref in enumerate((q0_ref, q1_ref)):
        reach = (slot + 1) * half
        span = slice(slot * half, reach)
        keys = all_keys[:reach]
        present = row_seg_ref[span, :] >= 0
        for head in range(QPK):
            cols = slice(head * HD, (head + 1) * HD)
            scores = lax.dot_general(
                q_ref[0, :, cols], keys, (((1,), (1,)), ((), ())),
                preferred_element_type=jnp.float32,
            )
            scores = scores + bias_ref[span, :reach]
            top = jnp.max(scores, axis=1, keepdims=True)
            raised = jnp.exp2((scores - top) * factor).astype(jnp.bfloat16)
            mixed = jnp.dot(raised, v_wide[:reach], preferred_element_type=jnp.float32)
            result = mixed[:, :HD] / mixed[:, HD:]
            out_ref[span, cols] = jnp.where(present, result, 0.0).astype(jnp.bfloat16)


def attend(sources, q3, kv3, slot_segment):
    half = q3.shape[1]
    rows = CAP * half
    width = QPK * HD

    def chosen(slot, base, size):
        return pl.BlockSpec((1, half, size), lambda g, src: (src[slot], 0, base + g))

    return pl.pallas_call(
        attention_kernel,
        out_shape=jax.ShapeDtypeStruct((rows, q3.shape[2]), jnp.bfloat16),
        grid_spec=pltpu.PrefetchScalarGridSpec(
            num_scalar_prefetch=1,
            grid=(KVH,),
            in_specs=[
                pl.BlockSpec((rows, 1), lambda g, src: (0, 0)),
                pl.BlockSpec((1, rows), lambda g, src: (0, 0)),
                chosen(0, 0, width), chosen(1, 0, width),
                chosen(0, 0, HD), chosen(1, 0, HD),
                chosen(0, KVH, HD), chosen(1, KVH, HD),
            ],
            out_specs=pl.BlockSpec((rows, width), lambda g, src: (0, g)),
            scratch_shapes=[pltpu.VMEM((rows, rows), jnp.float32)],
        ),
        compiler_params=pltpu.CompilerParams(vmem_limit_bytes=32 * 1024 * 1024),
    )(sources, slot_segment[:, None], slot_segment[None, :], q3, q3, kv3, kv3, kv3, kv3)


def slot_sources(target_device, target_slot):
    cycle_size = target_device.shape[0]
    own_index = lax.axis_index("shard")
    near = (own_index + jnp.array([0, -1, 1], jnp.int32)) % cycle_size
    lands = target_device[near] == own_index
    hits = jnp.logical_and(
        lands[None, :], target_slot[near][None, :] == jnp.arange(CAP, dtype=jnp.int32)[:, None]
    )
    return jnp.sum(jnp.where(hits, jnp.arange(3, dtype=jnp.int32)[None, :], 0), axis=1)


def per_device(
    mesh_shape,
    hidden,
    queries,
    segment,
    target_device,
    target_slot,
    key_codes,
    key_scales,
    value_codes,
    value_scales,
):
    slot_segment = slot_segments(segment, target_device, target_slot)
    sources = slot_sources(target_device, target_slot)
    q3, kv3 = gather_project(
        mesh_shape, hidden, queries, key_codes, key_scales, value_codes, value_scales
    )
    return attend(sources, q3, kv3, slot_segment)


def solution(mesh):
    return jax.shard_map(
        functools.partial(per_device, dict(mesh.shape)),
        mesh=mesh,
        in_specs=(
            P(("groups", "shard"), None),
            P(("groups", "shard"), None),
            P("groups"),
            P("groups"),
            P("groups"),
            P("shard", None),
            P("shard", None),
            P("shard", None),
            P("shard", None),
        ),
        out_specs=P(("groups", "shard"), None),
        check_vma=False,
    )
```

time: 208 us -> 157 us (0.75)
  waiting for transfers between devices: 147 us -> 0 us
  Pallas kernels: 11.5 us -> 141 us
  between operations: 15.5 us -> 0.05 us
  matrix products: 7.61 us -> 0 us
  other arithmetic: 8.73 us -> 2.4 us
  starting transfers between devices: 4.64 us -> 0 us
    all_gather x1 -> x0, waiting for transfers between devices: 133 us -> none  [per_device(): lax.all_gather(local_weights, 'shard', axis=0, tiled=True, axis_index_gro...]
    pallas_call x1 -> x2, Pallas kernels: 11.5 us -> 141 us  [the longest x1 128 us: gather_project(): pl.pallas_call(functools.partial(gather_kernel, chips, snake), out_shape=...]
    ppermute x6 -> x0, waiting for transfers between devices: 14.3 us -> none  [the longest x4 10.3 us: passed_along(): return lax.ppermute(block, axis, route)]
    dot_general x1 -> x0, matrix products: 7.61 us -> none  [projector(): return jnp.dot(hidden_rows, portion, preferred_element_type=jnp.float32)]
    ppermute x6 -> x0, starting transfers between devices: 4.64 us -> none  [the longest x4 3.37 us: passed_along(): return lax.ppermute(block, axis, route)]
    dynamic_slice x2 -> x0, local copies, waits for them, and re-layouts: 3.22 us -> none  [the longest x1 2.54 us: per_device(): lax.dynamic_index_in_dim(columns, core, 2, keepdims=False)]
    select_n x2 -> x1, other arithmetic: 3.72 us -> 0.67 us  [slot_sources(): lands = target_device[near] == own_index]
    gather x0 -> x2, local copies, waits for them, and re-layouts: none -> 2.59 us  [the longest x1 1.3 us: slot_sources(): target_slot[near][None, :] == jnp.arange(CAP, dtype=jnp.int32)[:, None]]
  transfers between devices with their start and end apart: 7 -> 0, of which waited for: 4 -> 0; matrix products, arithmetic and copies ran while one was open for 12% -> 0% of each run, Pallas kernels for 0% -> 0%
where the time goes in v2:
time: 157 us
  Pallas kernels  141 us (90%)
  local copies, waits for them, and re-layouts  13.5 us (9%)
  other arithmetic  2.4 us (2%)
    pallas_call x1, Pallas kernels, gather_project(): pl.pallas_call(functools.partial(gather_kernel, chips, snake), out_shape=...  128 us
    pallas_call x1, Pallas kernels, attend(): pl.pallas_call(attention_kernel, out_shape=jax.ShapeDtypeStruct((rows, q3...  12.2 us
    unnamed x16, local copies, waits for them, and re-layouts  10.2 us

profile of v2, /device:TPU:1, one launch (start us, length us, event | category | flops | bytes accessed | tf_op | source)
XLA Modules:
  0.0 156.6 jit_solution(2501894521565860084)
XLA Ops:
  0.0 0.7 compare_select_fusion
  0.7 0.7 broadcast_compare_fusion
  1.3 0.8 fusion.2
  2.1 1.3 gather_fusion.1
  3.4 1.3 gather_fusion
  4.7 0.1 fusion.source_ref
  4.8 0.7 broadcast_in_dim.64
  5.6 0.1 select_reduce_fusion
  5.6 0.1 select_bitcast_fusion
  5.7 0.1 copy.14
  5.9 0.0 copy-start.1
  5.9 2.2 %copy-done.1 = bf16[256,8192]{1,0:T(8,128)(2,1)S(1)} copy-done((bf16[256,8192]{1,0:T(8,128)(2,1)S(1)}, bf16[256,8192]{1,0:T(8,128)(2,1)}, u32[]{:S(2)}) %copy-start.1) | copy-done | bytes 4194328
  8.1 0.0 copy-start.2
  8.1 1.6 %copy-done.2 = bf16[256,4096]{1,0:T(8,128)(2,1)S(1)} copy-done((bf16[256,4096]{1,0:T(8,128)(2,1)S(1)}, bf16[256,4096]{1,0:T(8,128)(2,1)}, u32[]{:S(2)}) %copy-start.2) | copy-done | bytes 2097176
  9.7 0.0 copy-start.3
  9.7 1.0 copy-done.3
  10.7 0.0 copy-start.4
  10.7 1.0 copy-done.4
  11.8 0.0 copy-start.5
  11.8 0.7 copy-done.5
  12.4 0.0 copy-start.6
  12.4 0.7 copy-done.6
  13.1 128.5 %shard_map.100 = (bf16[3,256,4096]{2,1,0:T(8,128)(2,1)}, bf16[3,256,1024]{2,1,0:T(8,128)(2,1)S(1)}) custom-call(bf16[256,8192]{1,0:T(8,128)(2,1)S(1)} %copy-done.1, bf16[256,4096]{1,0:T(8,128)(2,1)S(1)} %copy-done.2, bf16[512,512]{1,0:T(8,128)(2,1)S(1)} %copy-done.3, bf16[512,512]{1,0:T(8,128)(2,1)S(1)} %copy-done.4, f32[4,4]{1,0:T(4,128)S(1)} %copy-done.5, ...), custom_call_target="tpu_custom_call" | custom-call | flops 4294967296 | bytes 33554432 | tf_op jit(solution)/shard_map/pallas_call | solution.py:243
  141.6 0.0 copy-start
  141.6 2.8 %copy-done = bf16[3,256,4096]{2,1,0:T(8,128)(2,1)S(1)} copy-done((bf16[3,256,4096]{2,1,0:T(8,128)(2,1)S(1)}, bf16[3,256,4096]{2,1,0:T(8,128)(2,1)}, u32[]{:S(2)}) %copy-start) | copy-done | bytes 6291480
  144.4 12.2 %shard_map.101 = bf16[512,4096]{1,0:T(8,128)(2,1)} custom-call(s32[2]{0:T(128)S(1)} %fusion.source_ref, s32[512,1]{1,0:T(8,128)S(1)} %bitcast.8, s32[1,512]{1,0:T(1,128)S(1)} %bitcast.10, bf16[3,256,4096]{2,1,0:T(8,128)(2,1)S(1)} %copy-done, bf16[3,256,4096]{2,1,0:T(8,128)(2,1)S(1)} %copy-done, ...), custom_call_target="tpu_custom_call" | custom-call | tf_op jit(solution)/shard_map/pallas_call | solution.py:318
  (3 shorter events, 0.0 us)
Async XLA Ops:
  5.9 2.2 %copy-start.1 = (bf16[256,8192]{1,0:T(8,128)(2,1)S(1)}, bf16[256,8192]{1,0:T(8,128)(2,1)}, u32[]{:S(2)}) copy-start(bf16[256,8192]{1,0:T(8,128)(2,1)} %hidden_ref.1) | copy-start | bytes 12582916
  8.1 1.6 %copy-start.2 = (bf16[256,4096]{1,0:T(8,128)(2,1)S(1)}, bf16[256,4096]{1,0:T(8,128)(2,1)}, u32[]{:S(2)}) copy-start(bf16[256,4096]{1,0:T(8,128)(2,1)} %queries_ref.1) | copy-start | bytes 6291460
  9.7 1.0 copy-start.3
  10.7 1.0 copy-start.4
  11.8 0.7 copy-start.5
  12.4 0.7 copy-start.6
  141.6 2.8 %copy-start = (bf16[3,256,4096]{2,1,0:T(8,128)(2,1)S(1)}, bf16[3,256,4096]{2,1,0:T(8,128)(2,1)}, u32[]{:S(2)}) copy-start(bf16[3,256,4096]{2,1,0:T(8,128)(2,1)} %get-tuple-element.7.q0_ref.q1_ref) | copy-start | bytes 18874372
